TPU v7x, 512 devices: a whole 4x8x8 slice. The times are simulated.
512 devices in a mesh: row: 16 (over x_lo, y), col: 8 (over z), layer: 4 (over x_hi, core).
Axes of the slice: x: 4 (x_hi: 2, x_lo: 2; x = x_hi * 2 + x_lo), y: 8, z: 8, core: 2. Of those that a mesh axis runs over, the one named last changes fastest.
Arguments:
- edge_values: bfloat16 [8192, 8192], P('row', ('col', 'layer')), as said below
- tile_pattern: int32 [64, 64], P('row', ('col', 'layer')), may hold values from 0 to 1, as said below
Outputs:
- motif: float32 [8192, 8192], P('row', ('col', 'layer'))
Inputs may be any that keep to these rules, and one draw needn't show every extreme that they name: `tile_pattern`: 1 marks a stored tile, 0 an empty one; the tiles on the diagonal are always stored; any other tile may be stored, and a tile row or tile column may be stored in full. `edge_values`: edge weights are nonnegative.
All inputs are finite; a program needn't handle non-finite values.
Results may differ from a plain program's by a relative error of at most 0.0003.
Values may be sent and summed in bfloat16 or wider, within the bound.
A program may use at most 64 MiB of HBM per device.

v0:
```python
import jax
import jax.numpy as jnp
from jax import lax
from jax.sharding import PartitionSpec as P


def masked(edge_values, tile_pattern):
    tile_rows, tile_cols = tile_pattern.shape
    height, breadth = edge_values.shape
    tile_size = height // tile_rows
    blocks = edge_values.reshape(tile_rows, tile_size, tile_cols, tile_size)
    keeper = tile_pattern.astype(jnp.bfloat16)[:, None, :, None]
    return (blocks * keeper).reshape(height, breadth)


def shards(edge_values, tile_pattern):
    adjacency = masked(edge_values, tile_pattern)
    column_strip = lax.all_gather(adjacency, "row", axis=0, tiled=True)
    paths = jnp.dot(
        lax.all_gather(adjacency, ("col", "layer"), axis=1, tiled=True),
        column_strip,
        preferred_element_type=jnp.float32,
    )
    return paths * adjacency.astype(jnp.float32)


def solution(mesh):
    return jax.shard_map(
        shards,
        mesh=mesh,
        in_specs=(P("row", ("col", "layer")), P("row", ("col", "layer"))),
        out_specs=P("row", ("col", "layer")),
        check_vma=False,
    )
```

profile of v0, /device:TPU:1, one launch (start us, length us, event | category | flops | bytes accessed | tf_op | source)
XLA Modules:
  0.0 224.6 jit_solution(3400265457739097103)
XLA Ops:
  6.5 0.0 all-gather.5.cloned.1.call-start
  6.5 0.7 convert_element_type.6
  7.2 0.1 copy.3
  7.3 0.2 mul.14
  7.5 1.7 bitcast_multiply_fusion
  9.3 0.0 all-gather.5.cloned.1.call-update
  9.3 0.0 all-gather.3.cloned.1.call-start
  9.3 0.7 all-gather.3.cloned.1.call-update
  10.0 75.3 %all-gather.5.cloned.1.call-done = bf16[8192,256]{1,0:T(8,128)(2,1)} async-done(((bf16[512,256]{1,0:T(8,128)(2,1)}), bf16[8192,256]{1,0:T(8,128)(2,1)}) %all-gather.5.cloned.1.call-update) | async-done | bytes 4194320 | tf_op jit(solution)/shard_map/all_gather | solution.py:18
  85.4 124.6 %all-gather.3.cloned.1.call-done = bf16[512,8192]{1,0:T(8,128)(2,1)} async-done(((bf16[512,256]{1,0:T(8,128)(2,1)}), bf16[512,8192]{1,0:T(8,128)(2,1)}) %all-gather.3.cloned.1.call-update) | async-done | bytes 8388624 | tf_op jit(solution)/shard_map/all_gather | solution.py:20
  209.9 7.8 %convolution_multiply_fusion = f32[512,256]{1,0:T(8,128)} fusion(bf16[512,8192]{1,0:T(8,128)(2,1)} %all-gather.3.cloned.1.call-done, bf16[8192,256]{1,0:T(8,128)(2,1)} %all-gather.5.cloned.1.call-done, bf16[512,256]{1,0:T(8,128)(2,1)} %bitcast_multiply_fusion), kind=kOutput, calls=%fused_computation | convolution fusion | flops 2147745792 | bytes 13369344 | tf_op jit(solution)/shard_map/dot_general | solution.py:19
Async XLA Ops:
  6.5 78.8 %all-gather.5.cloned.1.call-start = ((), (), s32[]{:S(2)}) async-start(), calls=%async_computation.1 | async-start | bytes 4456448 | tf_op jit(solution)/shard_map/all_gather | solution.py:18
  9.3 200.7 %all-gather.3.cloned.1.call-start = ((), (), s32[]{:S(2)}) async-start(), calls=%async_computation | async-start | bytes 8650752 | tf_op jit(solution)/shard_map/all_gather | solution.py:20
Sparse Core Ops, SparseCore 0:
  9.4 75.8 all-gather.4
  88.5 121.3 all-gather.2
where the time goes:
time: 225 us
  waiting for transfers between devices  201 us (89%)
  between operations  13.4 us (6%)
  matrix products  7.78 us (3%)
  other arithmetic  2.39 us (1%)
    all_gather x1, waiting for transfers between devices, shards(): lax.all_gather(adjacency, ('col', 'layer'), axis=1, tiled=True)  125 us
    all_gather x1, waiting for transfers between devices, shards(): column_strip = lax.all_gather(adjacency, 'row', axis=0, tiled=True)  75.3 us
    dot_general x1, matrix products, shards(): jnp.dot(lax.all_gather(adjacency, ('col', 'layer'), axis=1, tiled=True),...  7.78 us
  transfers between devices with their start and end apart: 2, of which 2 were waited for; matrix products, arithmetic and copies ran while one was open for 0% of the time, Pallas kernels for 0%

commit v1 on v0

v1 whole, which is shorter than its diff:
```python
import functools

import jax
import jax.numpy as jnp
from jax import lax
from jax.experimental import pallas as pl
from jax.experimental.pallas import tpu as pltpu
from jax.sharding import PartitionSpec as P

MESH = pl.DeviceIdType.MESH
PARTS = 2
RING = 8


def wrap(d):
    return (d + RING // 2 - 1) % RING - (RING // 2 - 1)


def plan():
    flows = {}

    def add(flow, source, target):
        flows.setdefault(flow, []).append((flow, source, target))

    up = [(0, 0), (0, 1), (0, 2), (0, 3), (1, 0), (1, 2)]
    down = [(0, 0), (0, -1), (0, -2), (1, 0), (1, -1), (1, -2)]
    for side, d in up:
        for s in range(PARTS):
            add("ym", ("C", side, d, s), ("C", side, wrap(d + 1), s))
            add("zm", ("R", side, d, 0, s), ("R", side, wrap(d + 1), 0, s))
    for side, d in down:
        for s in range(PARTS):
            add("yp", ("C", side, d, s), ("C", side, wrap(d - 1), s))
            add("zp", ("R", side, d, 0, s), ("R", side, wrap(d - 1), 0, s))
    for d in (0, 2, 4):
        for s in range(PARTS):
            add("lo", ("C", 0, d, s), ("C", 1, d, s))
            add("hi", ("R", 0, d, 0, s), ("R", 1, d, 0, s))
    return flows


RATE = {"sib": 300e3}


def schedule(flows):
    flows = {name: list(copies) for name, copies in flows.items()}
    size = 512 * 256 * 2 / PARTS
    ready = {}
    for side in (0,):
        for s in range(PARTS):
            ready["C", 0, 0, s] = 0.0
            ready["R", 0, 0, 0, s] = 0.0
    free = {}
    done, order = set(), []
    pending = {name: 0 for name in flows}
    shared = []
    for s in range(PARTS):
        shared.append((0.0, ("R", 0, 0, 0, s)))
    while any(pending[name] < len(flows[name]) for name in flows):
        best = None
        for name in flows:
            if pending[name] < len(flows[name]):
                copy = flows[name][pending[name]]
                if copy[1] in ready:
                    at = ready[copy[1]]
                    if best is None or (at, free.get(name, 0.0)) < best[:2]:
                        best = (at, free.get(name, 0.0), name, copy)
        at, _, name, copy = best
        start = max(at, free.get(name, 0.0))
        end = start + size / RATE.get(name, 50e3) + (1.0 if name != "hi" else 1.5)
        free[name] = end - 1.0
        ready[copy[2]] = end
        order.append((at, copy))
        pending[name] += 1
    for piece, at in ready.items():
        if piece[0] == "R":
            _, h, d, _, s = piece
            order.append((at + 0.01, ("sib", piece, ("R", h, d, 1, s))))
    order.sort(key=lambda entry: entry[0])
    return [copy for _, copy in order]


def kernel(copies, edge_ref, tile_ref, out_ref, rows_ref, cols_ref, total_ref, send_sem, recv_sem):
    row, z, layer = lax.axis_index("row"), lax.axis_index("col"), lax.axis_index("layer")
    x_lo, y = row // RING, row % RING
    x_hi, core = layer // 2, layer % 2
    height, breadth = edge_ref.shape
    part = height // PARTS

    def turn(a, d):
        return (a + (d + RING)) % RING

    devices = {
        "yp": (x_lo * RING + turn(y, 1), z, layer),
        "ym": (x_lo * RING + turn(y, -1), z, layer),
        "zp": (row, turn(z, 1), layer),
        "zm": (row, turn(z, -1), layer),
        "lo": ((1 - x_lo) * RING + y, z, layer),
        "hi": (row, z, (1 - x_hi) * 2 + core),
        "sib": (row, z, x_hi * 2 + 1 - core),
    }
    barrier = pltpu.get_barrier_semaphore()
    for device in devices.values():
        pl.semaphore_signal(barrier, inc=1, device_id=device, device_id_type=MESH)

    tile_rows, tile_cols = tile_ref.shape
    tile = height // tile_rows
    me_r = z * 4 + layer
    for i in range(tile_rows):
        for j in range(tile_cols):
            keeper = tile_ref[i, j].astype(jnp.float32)
            at = (pl.ds(i * tile, tile), pl.ds(j * tile, tile))
            block = (edge_ref[at].astype(jnp.float32) * keeper).astype(jnp.bfloat16)
            rows_ref[(me_r, *at)] = block
            cols_ref[(row, *at)] = block
    pl.semaphore_wait(barrier, len(devices))

    def place(piece):
        span = pl.ds(piece[-1] * part, part)
        if piece[0] == "C":
            _, side, d, _ = piece
            index = (x_lo if side == 0 else 1 - x_lo) * RING + turn(y, d)
            return cols_ref.at[index, span]
        _, h, d, k, _ = piece
        index = turn(z, d) * 4 + (x_hi if h == 0 else 1 - x_hi) * 2 + (core if k == 0 else 1 - core)
        return rows_ref.at[index, span]

    arrivals = {copy[2]: n for n, copy in enumerate(copies)}
    waited = set()

    def arrive(piece):
        if piece not in arrivals or piece in waited:
            return
        waited.add(piece)
        n = arrivals[piece]
        there = place(piece)
        pltpu.make_async_remote_copy(
            src_ref=there, dst_ref=there, send_sem=send_sem.at[n], recv_sem=recv_sem.at[n],
            device_id=devices[copies[n][0]], device_id_type=MESH,
        ).wait_recv()

    started = []
    for n, (flow, source, _) in enumerate(copies):
        arrive(source)
        here = place(source)
        copy = pltpu.make_async_remote_copy(
            src_ref=here, dst_ref=here, send_sem=send_sem.at[n], recv_sem=recv_sem.at[n],
            device_id=devices[flow], device_id_type=MESH,
        )
        copy.start()
        started.append(copy)
    for _, _, target in copies:
        arrive(target)

    half = height // 2
    for m in range(2):
        span = pl.ds(m * half, half)
        total_ref[span, :] = jnp.zeros((half, breadth), jnp.float32)

        def step(j, carry):
            depth = pl.ds((j % 2) * breadth, breadth)
            total_ref[span, :] += jnp.dot(
                rows_ref[j, span, :], cols_ref[j // 2, depth, :], preferred_element_type=jnp.float32
            )
            return carry

        lax.fori_loop(0, rows_ref.shape[0], step, 0)
    out_ref[...] = total_ref[...] * cols_ref[row].astype(jnp.float32)
    for copy in started:
        copy.wait_send()


def shards(edge_values, tile_pattern):
    height, breadth = edge_values.shape
    copies = schedule(plan())
    return pl.pallas_call(
        functools.partial(kernel, copies),
        out_shape=jax.ShapeDtypeStruct((height, breadth), jnp.float32),
        in_specs=[pl.BlockSpec(memory_space=pltpu.VMEM), pl.BlockSpec(memory_space=pltpu.SMEM)],
        out_specs=pl.BlockSpec(memory_space=pltpu.VMEM),
        scratch_shapes=[
            pltpu.VMEM((32, height, breadth), jnp.bfloat16),
            pltpu.VMEM((16, height, breadth), jnp.bfloat16),
            pltpu.VMEM((height, breadth), jnp.float32),
            pltpu.SemaphoreType.DMA((len(copies),)),
            pltpu.SemaphoreType.DMA((len(copies),)),
        ],
        compiler_params=pltpu.CompilerParams(
            collective_id=0, has_side_effects=True, vmem_limit_bytes=24 * 1024 * 1024
        ),
        cost_estimate=pl.CostEstimate(flops=2 * height * 8192 * breadth, bytes_accessed=1 << 20, transcendentals=0),
    )(edge_values, tile_pattern)


def solution(mesh):
    return jax.shard_map(
        shards,
        mesh=mesh,
        in_specs=(P("row", ("col", "layer")), P("row", ("col", "layer"))),
        out_specs=P("row", ("col", "layer")),
        check_vma=False,
    )
```

time: 225 us -> 78.7 us (0.35)
  waiting for transfers between devices: 201 us -> 0 us
  Pallas kernels: 0 us -> 76 us
  between operations: 13.4 us -> 0.01 us
  matrix products: 7.78 us -> 0 us
  other arithmetic: 2.39 us -> 0 us
    all_gather x2 -> x0, waiting for transfers between devices: 200 us -> none  [the longest x1 125 us: shards(): lax.all_gather(adjacency, ('col', 'layer'), axis=1, tiled=True)]
    pallas_call x0 -> x1, Pallas kernels: none -> 76 us  [shards(): pl.pallas_call(functools.partial(kernel, copies), out_shape=jax.ShapeDtyp...]
    dot_general x1 -> x0, matrix products: 7.78 us -> none  [shards(): jnp.dot(lax.all_gather(adjacency, ('col', 'layer'), axis=1, tiled=True),...]
    unnamed x0 -> x4, local copies, waits for them, and re-layouts: none -> 2.51 us
  transfers between devices with their start and end apart: 2 -> 0, of which waited for: 2 -> 0; matrix products, arithmetic and copies ran while one was open for 0% -> 0% of each run, Pallas kernels for 0% -> 0%
where the time goes in v1:
time: 78.7 us; the launch traced here: 78.5 us
  Pallas kernels  76 us (97%)
  local copies, waits for them, and re-layouts  2.51 us (3%)
    pallas_call x1, Pallas kernels, shards(): pl.pallas_call(functools.partial(kernel, copies), out_shape=jax.ShapeDtyp...  76 us
    unnamed x4, local copies, waits for them, and re-layouts  2.51 us

profile of v1, /device:TPU:1, one launch (start us, length us, event | category | flops | bytes accessed | tf_op | source)
XLA Modules:
  0.0 78.5 jit_solution(864821671796183526)
XLA Ops:
  0.0 0.8 copy.3.tile_ref
  0.8 0.0 copy-start
  0.8 0.9 %copy-done = bf16[512,256]{1,0:T(8,128)(2,1)S(1)} copy-done((bf16[512,256]{1,0:T(8,128)(2,1)S(1)}, bf16[512,256]{1,0:T(8,128)(2,1)}, u32[]{:S(2)}) %copy-start) | copy-done | bytes 262168
  1.7 76.0 %shard_map.28 = f32[512,256]{1,0:T(8,128)S(1)} custom-call(bf16[512,256]{1,0:T(8,128)(2,1)S(1)} %copy-done, s32[4,2]{1,0:T(4,128)S(1)} %copy.3.tile_ref), custom_call_target="tpu_custom_call" | custom-call | flops 2147483648 | bytes 1048576 | tf_op jit(solution)/shard_map/pallas_call | solution.py:176
  77.7 0.8 %copy.5 = f32[512,256]{1,0:T(8,128)} copy(f32[512,256]{1,0:T(8,128)S(1)} %shard_map.28) | data formatting | bytes 1048576
Async XLA Ops:
  0.8 0.9 %copy-start = (bf16[512,256]{1,0:T(8,128)(2,1)S(1)}, bf16[512,256]{1,0:T(8,128)(2,1)}, u32[]{:S(2)}) copy-start(bf16[512,256]{1,0:T(8,128)(2,1)} %edge_ref.1) | copy-start | bytes 786436

commit v2 on v1

v2 whole, which is shorter than its diff:
```python
import jax
import jax.numpy as jnp
from jax import lax
from jax.experimental import pallas as pl
from jax.experimental.pallas import tpu as pltpu
from jax.sharding import PartitionSpec as P

MESH = pl.DeviceIdType.MESH
RING = 8
PARTS = 2
FLOWS = {
    "ym": ("C", 0, 1), "yp": ("C", 0, -1), "lo": ("C", 1, 0),
    "zm": ("R", 0, 1), "zp": ("R", 0, -1), "hi": ("R", 1, 0),
}
STEPS = (
    ("ym", 0, 0, 0), ("yp", 0, 0, 0), ("zm", 0, 0, 0), ("zp", 0, 0, 0), ("lo", 0, 0, 0), ("ym", 0, 0, 1),
    ("yp", 0, 0, 1), ("zm", 0, 0, 1), ("zp", 0, 0, 1), ("lo", 0, 0, 1), ("hi", 0, 0, 0), ("sib", 0, 0, 0),
    ("sib", 0, 0, 1), ("ym", 0, 1, 0), ("yp", 0, -1, 0), ("sib", 0, 1, 0), ("zm", 0, 1, 0), ("sib", 0, -1, 0),
    ("zp", 0, -1, 0), ("ym", 1, 0, 0), ("yp", 1, 0, 0), ("hi", 0, -1, 0), ("ym", 0, 1, 1), ("yp", 0, -1, 1),
    ("sib", 0, 1, 1), ("zm", 0, 1, 1), ("sib", 0, -1, 1), ("zp", 0, -1, 1), ("hi", 0, -1, 1), ("ym", 1, 0, 1),
    ("yp", 1, 0, 1), ("sib", 0, 2, 0), ("lo", 0, -2, 0), ("sib", 0, -2, 0), ("zm", 0, 2, 0), ("zp", 0, -2, 0),
    ("sib", 1, 0, 0), ("zm", 1, 0, 0), ("ym", 0, 2, 0), ("yp", 0, -2, 0), ("sib", 0, 2, 1), ("hi", 0, -2, 0),
    ("sib", 0, -2, 1), ("zm", 0, 2, 1), ("zp", 0, -2, 1), ("mul", 131, 387), ("sib", 1, -1, 0), ("ym", 1, 1, 0),
    ("yp", 0, -2, 1), ("sib", 0, 3, 0), ("zm", 0, 3, 0), ("sib", 0, -3, 0), ("hi", 0, 3, 0), ("sib", 1, -1, 1),
    ("zp", 1, -1, 1), ("ym", 0, 2, 1), ("zm", 1, -1, 1), ("yp", 1, -1, 1), ("sib", 1, 1, 0), ("lo", 0, 2, 1),
    ("sib", 0, -3, 1), ("zp", 0, -3, 1), ("mul", 32967, 33735), ("yp", 1, -2, 0), ("zm", 1, 1, 0),
    ("ym", 0, 3, 0), ("sib", 0, 3, 1), ("lo", 0, 3, 0), ("sib", 1, -2, 1), ("zp", 1, -2, 1), ("sib", 1, -2, 0),
    ("zp", 1, -2, 0), ("yp", 0, -3, 1), ("sib", 0, 4, 0), ("hi", 0, 3, 1), ("sib", 0, 4, 1), ("sib", 1, 3, 0),
    ("zm", 1, 3, 0), ("mul", 49391, 33767), ("yp", 1, -2, 1), ("sib", 1, 0, 1), ("zm", 1, 0, 1), ("sib", 1, -3, 1),
    ("zp", 1, -3, 1), ("ym", 1, 2, 1), ("hi", 0, 2, 1), ("yp", 1, -3, 0), ("sib", 1, 2, 0), ("sib", 1, -3, 0),
    ("mul", 49663, 51183), ("ym", 1, 3, 1), ("sib", 1, 4, 0), ("sib", 1, 4, 1), ("sib", 1, 3, 1),
    ("mul", 57855, 53247), ("sib", 1, 1, 1), ("sib", 1, 2, 1), ("mul", 63999, 61439), ("mul", 65535, 65535),
)


def wrap(d):
    return (d + RING // 2 - 1) % RING - (RING // 2 - 1)


def copies_of(steps):
    copies = []
    for flow, *rest in steps:
        if flow == "sib":
            side, d, s = rest
            copies.append((flow, ("R", side, d, 0, s), ("R", side, d, 1, s)))
        elif flow != "mul":
            side, d, s = rest
            kind, flip, shift = FLOWS[flow]
            core = (0,) if kind == "R" else ()
            copies.append((flow, (kind, side, d, *core, s), (kind, side ^ flip, wrap(d + shift), *core, s)))
    return copies


def kernel(edge_ref, tile_ref, out_ref, rows_ref, cols_ref, total_ref, send_sem, recv_sem):
    row, z, layer = lax.axis_index("row"), lax.axis_index("col"), lax.axis_index("layer")
    x_lo, y = row // RING, row % RING
    x_hi, core = layer // 2, layer % 2
    height, breadth = edge_ref.shape
    part = height // PARTS

    def turn(a, d):
        return (a + (d + RING)) % RING

    devices = {
        "yp": (x_lo * RING + turn(y, 1), z, layer),
        "ym": (x_lo * RING + turn(y, -1), z, layer),
        "zp": (row, turn(z, 1), layer),
        "zm": (row, turn(z, -1), layer),
        "lo": ((1 - x_lo) * RING + y, z, layer),
        "hi": (row, z, (1 - x_hi) * 2 + core),
        "sib": (row, z, x_hi * 2 + 1 - core),
    }
    barrier = pltpu.get_barrier_semaphore()
    for device in devices.values():
        pl.semaphore_signal(barrier, inc=1, device_id=device, device_id_type=MESH)

    tile_rows, tile_cols = tile_ref.shape
    tile = height // tile_rows
    mine = z * 4 + layer
    for i in range(tile_rows):
        for j in range(tile_cols):
            keeper = tile_ref[i, j].astype(jnp.float32)
            at = (pl.ds(i * tile, tile), pl.ds(j * tile, tile))
            block = (edge_ref[at].astype(jnp.float32) * keeper).astype(jnp.bfloat16)
            rows_ref[(mine, *at)] = block
            cols_ref[(row, *at)] = block
    total_ref[...] = jnp.zeros_like(total_ref)
    pl.semaphore_wait(barrier, len(devices))

    def place(piece):
        span = pl.ds(piece[-1] * part, part)
        if piece[0] == "C":
            _, side, d, _ = piece
            index = (x_lo if side == 0 else 1 - x_lo) * RING + turn(y, d)
            return cols_ref.at[index, span]
        _, side, d, k, _ = piece
        index = turn(z, d) * 4 + (x_hi if side == 0 else 1 - x_hi) * 2 + (core if k == 0 else 1 - core)
        return rows_ref.at[index, span]

    copies = copies_of(STEPS)
    arrivals = {copy[2]: n for n, copy in enumerate(copies)}
    waited = set()

    def arrive(piece):
        if piece not in arrivals or piece in waited:
            return
        waited.add(piece)
        n = arrivals[piece]
        there = place(piece)
        pltpu.make_async_remote_copy(
            src_ref=there, dst_ref=there, send_sem=send_sem.at[n], recv_sem=recv_sem.at[n],
            device_id=devices[copies[n][0]], device_id_type=MESH,
        ).wait_recv()

    def multiply(rows, cols, before):
        def step(k, carry):
            r = (k % 2 + x_hi) % 2 * RING + (k // 2 - z + RING) % RING
            c = (k // RING + x_lo) % 2 * RING + (k % RING - y + RING) % RING

            def both(masks):
                return ((masks[0] >> r) % 2) * ((masks[1] >> c) % 2)

            @pl.when(both((rows, cols)) - both(before) == 1)
            def _():
                left = jnp.concatenate([rows_ref[2 * k], rows_ref[2 * k + 1]], axis=1)
                total_ref[...] += jnp.dot(left, cols_ref[k], preferred_element_type=jnp.float32)

            return carry

        lax.fori_loop(0, cols_ref.shape[0], step, 0)

    order = {piece: n for n, piece in enumerate(copy[2] for copy in copies)}
    before, started = (0, 0), []
    for step in STEPS:
        if step[0] == "mul":
            _, rows, cols = step
            ready = [p for p in order if ((rows if p[0] == "R" else cols) >> (RING * p[1] + p[2] % RING)) % 2]
            for piece in ready:
                arrive(piece)
            multiply(rows, cols, before)
            before = (rows, cols)
            continue
        n = len(started)
        flow, source, _ = copies[n]
        arrive(source)
        here = place(source)
        copy = pltpu.make_async_remote_copy(
            src_ref=here, dst_ref=here, send_sem=send_sem.at[n], recv_sem=recv_sem.at[n],
            device_id=devices[flow], device_id_type=MESH,
        )
        copy.start()
        started.append(copy)
    out_ref[...] = total_ref[...] * cols_ref[row].astype(jnp.float32)
    for copy in started:
        copy.wait_send()


def shards(edge_values, tile_pattern):
    height, breadth = edge_values.shape
    count = len(copies_of(STEPS))
    return pl.pallas_call(
        kernel,
        out_shape=jax.ShapeDtypeStruct((height, breadth), jnp.float32),
        in_specs=[pl.BlockSpec(memory_space=pltpu.VMEM), pl.BlockSpec(memory_space=pltpu.SMEM)],
        out_specs=pl.BlockSpec(memory_space=pltpu.VMEM),
        scratch_shapes=[
            pltpu.VMEM((32, height, breadth), jnp.bfloat16),
            pltpu.VMEM((16, height, breadth), jnp.bfloat16),
            pltpu.VMEM((height, breadth), jnp.float32),
            pltpu.SemaphoreType.DMA((count,)),
            pltpu.SemaphoreType.DMA((count,)),
        ],
        compiler_params=pltpu.CompilerParams(
            collective_id=0, has_side_effects=True, vmem_limit_bytes=24 * 1024 * 1024
        ),
        cost_estimate=pl.CostEstimate(flops=2 * height * 8192 * breadth, bytes_accessed=1 << 20, transcendentals=0),
    )(edge_values, tile_pattern)


def solution(mesh):
    return jax.shard_map(
        shards,
        mesh=mesh,
        in_specs=(P("row", ("col", "layer")), P("row", ("col", "layer"))),
        out_specs=P("row", ("col", "layer")),
        check_vma=False,
    )
```

time: 78.7 us -> 57.7 us (0.73)
  Pallas kernels: 76 us -> 54.4 us
    pallas_call x1, Pallas kernels: 76 us -> 54.4 us  [shards(): pl.pallas_call(kernel, out_shape=jax.ShapeDtypeStruct((height, breadth),...]
where the time goes in v2:
time: 57.7 us; the launch traced here: 57 us
  Pallas kernels  54.4 us (94%)
  local copies, waits for them, and re-layouts  2.51 us (4%)
    pallas_call x1, Pallas kernels, shards(): pl.pallas_call(kernel, out_shape=jax.ShapeDtypeStruct((height, breadth),...  54.4 us
    unnamed x4, local copies, waits for them, and re-layouts  2.51 us

profile of v2, /device:TPU:1, one launch (start us, length us, event | category | flops | bytes accessed | tf_op | source)
XLA Modules:
  0.0 57.0 jit_solution(9902226858087284905)
XLA Ops:
  0.0 0.8 %copy.3.tile_ref = s32[4,2]{1,0:T(4,128)S(1)} copy(s32[4,2]{0,1:T(2,128)} %param.3) | data formatting | bytes 64 | tf_op args[1]
  0.8 0.0 copy-start
  0.8 0.9 %copy-done = bf16[512,256]{1,0:T(8,128)(2,1)S(1)} copy-done((bf16[512,256]{1,0:T(8,128)(2,1)S(1)}, bf16[512,256]{1,0:T(8,128)(2,1)}, u32[]{:S(2)}) %copy-start) | copy-done | bytes 262168
  1.7 54.4 %shard_map.28 = f32[512,256]{1,0:T(8,128)S(1)} custom-call(bf16[512,256]{1,0:T(8,128)(2,1)S(1)} %copy-done, s32[4,2]{1,0:T(4,128)S(1)} %copy.3.tile_ref), custom_call_target="tpu_custom_call" | custom-call | flops 2147483648 | bytes 1048576 | tf_op jit(solution)/shard_map/pallas_call | solution.py:161
  56.2 0.8 %copy.5 = f32[512,256]{1,0:T(8,128)} copy(f32[512,256]{1,0:T(8,128)S(1)} %shard_map.28) | data formatting | bytes 1048576
Async XLA Ops:
  0.8 0.9 %copy-start = (bf16[512,256]{1,0:T(8,128)(2,1)S(1)}, bf16[512,256]{1,0:T(8,128)(2,1)}, u32[]{:S(2)}) copy-start(bf16[512,256]{1,0:T(8,128)(2,1)} %edge_ref.1) | copy-start | bytes 786436

commit v3 on v2

v3 whole, which is shorter than its diff:
```python
import jax
import jax.numpy as jnp
from jax import lax
from jax.experimental import pallas as pl
from jax.experimental.pallas import tpu as pltpu
from jax.sharding import PartitionSpec as P

MESH = pl.DeviceIdType.MESH
RING = 8
CUTS = (0, 128, 256, 384, 512)
LAG = 64
FLOWS = {
    "ym": ("C", 0, 1), "yp": ("C", 0, -1), "lo": ("C", 1, 0),
    "zm": ("R", 0, 1), "zp": ("R", 0, -1), "hi": ("R", 1, 0),
}
STEPS = (
    ("ym", 0, 0, 0), ("yp", 0, 0, 0), ("zm", 0, 0, 0), ("zp", 0, 0, 0), ("lo", 0, 0, 0), ("ym", 0, 0, 1),
    ("yp", 0, 0, 1), ("zm", 0, 0, 1), ("zp", 0, 0, 1), ("lo", 0, 0, 1), ("ym", 0, 0, 2), ("yp", 0, 0, 2),
    ("zm", 0, 0, 2), ("zp", 0, 0, 2), ("lo", 0, 0, 2), ("ym", 0, 0, 3), ("yp", 0, 0, 3), ("zm", 0, 0, 3),
    ("zp", 0, 0, 3), ("lo", 0, 0, 3), ("sib", 0, 0, 0, 4), ("hi", 0, 0, 0), ("ym", 0, 1, 0), ("yp", 0, -1, 0),
    ("zm", 0, 1, 0), ("zp", 0, -1, 0), ("ym", 1, 0, 0), ("yp", 1, 0, 0), ("hi", 0, -1, 0), ("zm", 0, 1, 1),
    ("zp", 0, -1, 1), ("ym", 1, 0, 1), ("yp", 1, 0, 1), ("hi", 0, -1, 1), ("zm", 0, 1, 2), ("zp", 0, -1, 2),
    ("ym", 1, 0, 2), ("yp", 1, 0, 2), ("hi", 0, -1, 2), ("sib", 0, 1, 0, 4), ("zm", 0, 1, 3), ("sib", 0, -1, 0, 4),
    ("zp", 0, -1, 3), ("ym", 1, 0, 3), ("yp", 1, 0, 3), ("hi", 0, -1, 3), ("zm", 0, 2, 0), ("zp", 0, -2, 0),
    ("ym", 0, 2, 0), ("yp", 0, -2, 0), ("lo", 0, -2, 0), ("zm", 1, 0, 0), ("zp", 0, -2, 1), ("ym", 0, 1, 1),
    ("yp", 0, -1, 1), ("zm", 0, 2, 1), ("hi", 0, 2, 0), ("zp", 1, -1, 0), ("mul", 131, 387), ("ym", 0, 1, 2),
    ("yp", 1, -1, 1), ("zm", 0, 2, 2), ("zp", 0, -2, 2), ("hi", 0, 2, 1), ("sib", 0, 2, 0, 4), ("sib", 0, -2, 0, 4),
    ("ym", 0, 1, 3), ("yp", 1, -1, 2), ("zm", 1, -1, 1), ("zp", 1, -1, 1), ("hi", 0, 2, 2), ("sib", 0, -3, 0, 1),
    ("ym", 1, 1, 0), ("yp", 0, -1, 2), ("zm", 1, -1, 2), ("mul", 131, 33667), ("zp", 1, -1, 2), ("hi", 0, 2, 3),
    ("sib", 1, -1, 0, 4), ("sib", 0, -3, 1, 1), ("ym", 0, 3, 0), ("yp", 1, -1, 3), ("zm", 1, -1, 3),
    ("zp", 1, -1, 3), ("hi", 0, -3, 0), ("ym", 0, 2, 1), ("yp", 0, -2, 1), ("zm", 0, 2, 3), ("zp", 0, -3, 0),
    ("lo", 0, -3, 0), ("sib", 0, -3, 2, 1), ("ym", 0, 2, 2), ("mul", 32967, 33667), ("yp", 0, -1, 3),
    ("zm", 1, 2, 0), ("zp", 0, -3, 1), ("hi", 0, -3, 1), ("ym", 0, 2, 3), ("yp", 1, -2, 1), ("zm", 1, 2, 1),
    ("zp", 1, 2, 1), ("hi", 0, -3, 2), ("ym", 1, 1, 1), ("yp", 0, -2, 2), ("zm", 1, 2, 2), ("mul", 32967, 33671),
    ("zp", 1, 2, 2), ("lo", 0, 2, 2), ("sib", 1, 2, 0, 4), ("sib", 1, 0, 0, 4), ("sib", 1, -2, 0, 4),
    ("ym", 1, 1, 3), ("yp", 1, -2, 2), ("zm", 1, 2, 3), ("zp", 1, -2, 3), ("lo", 0, 4, 0), ("sib", 0, 3, 0, 4),
    ("sib", 0, 4, 0, 1), ("ym", 0, 3, 1), ("yp", 1, -2, 3), ("zm", 1, 0, 3), ("zp", 0, -3, 2), ("hi", 0, 4, 0),
    ("mul", 32967, 50055), ("sib", 0, 4, 1, 1), ("ym", 0, 3, 2), ("yp", 0, -2, 3), ("zm", 0, 3, 3),
    ("zp", 0, -2, 3), ("hi", 0, 4, 1), ("ym", 0, 3, 3), ("yp", 1, -3, 1), ("lo", 0, 3, 0), ("zp", 1, -3, 2),
    ("mul", 50639, 50127), ("ym", 1, 2, 1), ("lo", 0, 3, 2), ("yp", 1, -3, 2), ("sib", 1, 3, 0, 4),
    ("zm", 1, 3, 3), ("sib", 1, -3, 0, 4), ("mul", 50639, 50127), ("ym", 1, 2, 3), ("yp", 1, -3, 3),
    ("sib", 1, 1, 0, 4), ("sib", 0, 4, 2, 1), ("mul", 50639, 59343), ("sib", 1, 4, 0, 1), ("sib", 0, 4, 3, 1),
    ("sib", 0, -3, 3, 1), ("sib", 1, 4, 1, 1), ("sib", 1, 4, 3, 1), ("sib", 1, 4, 2, 1), ("mul", 61391, 59375),
    ("mul", 61439, 59391), ("mul", 65535, 65535),
)


def wrap(d):
    return (d + RING // 2 - 1) % RING - (RING // 2 - 1)


def copies_of(steps):
    copies = []
    for flow, *rest in steps:
        if flow == "sib":
            side, d, s, n = rest
            copies.append((flow, ("R", side, d, 0, (s, n)), ("R", side, d, 1, (s, n))))
        elif flow != "mul":
            side, d, s = rest
            kind, flip, shift = FLOWS[flow]
            core = (0,) if kind == "R" else ()
            copies.append((flow, (kind, side, d, *core, s), (kind, side ^ flip, wrap(d + shift), *core, s)))
    return copies


def kernel(edge_hbm, tile_hbm, out_ref, edge_ref, tile_ref, turn_ref, rows_ref, cols_ref, total_ref, load_sem, send_sem, recv_sem):
    row, z, layer = lax.axis_index("row"), lax.axis_index("col"), lax.axis_index("layer")
    x_lo, y = row // RING, row % RING
    x_hi, core = layer // 2, layer % 2
    height, breadth = edge_ref.shape

    def turn(a, d):
        return (a + (d + RING)) % RING

    devices = {
        "yp": (x_lo * RING + turn(y, 1), z, layer),
        "ym": (x_lo * RING + turn(y, -1), z, layer),
        "zp": (row, turn(z, 1), layer),
        "zm": (row, turn(z, -1), layer),
        "lo": ((1 - x_lo) * RING + y, z, layer),
        "hi": (row, z, (1 - x_hi) * 2 + core),
        "sib": (row, z, x_hi * 2 + 1 - core),
    }
    barrier = pltpu.get_barrier_semaphore()
    for device in devices.values():
        pl.semaphore_signal(barrier, inc=1, device_id=device, device_id_type=MESH)

    loads = [
        pltpu.make_async_copy(tile_hbm, tile_ref, load_sem.at[0]),
        pltpu.make_async_copy(edge_hbm, edge_ref, load_sem.at[1]),
    ]
    for load in loads:
        load.start()
    for load in loads:
        load.wait()
    tile_cols, tile_rows = tile_ref.shape
    tile = height // tile_rows
    mine = z * 4 + layer
    for i in range(tile_rows):
        for j in range(tile_cols):
            stored = tile_ref[j, i] == 1
            at = (pl.ds(i * tile, tile), pl.ds(j * tile, tile))
            block = edge_ref[at]
            block = jnp.where(stored, block, jnp.zeros_like(block))
            rows_ref[(mine, *at)] = block
            cols_ref[(row, *at)] = block
    pl.semaphore_wait(barrier, len(devices))

    def place(piece):
        first, parts = piece[-1] if isinstance(piece[-1], tuple) else (piece[-1], 1)
        span = pl.ds(CUTS[first], CUTS[first + parts] - CUTS[first])
        if piece[0] == "C":
            _, side, d, _ = piece
            index = (x_lo if side == 0 else 1 - x_lo) * RING + turn(y, d)
            return cols_ref.at[index, span]
        _, side, d, k, _ = piece
        index = turn(z, d) * 4 + (x_hi if side == 0 else 1 - x_hi) * 2 + (core if k == 0 else 1 - core)
        return rows_ref.at[index, span]

    copies = copies_of(STEPS)
    arrivals = {copy[2]: n for n, copy in enumerate(copies)}
    waited = set()

    def arrive(piece):
        if piece not in arrivals or piece in waited:
            return
        waited.add(piece)
        n = arrivals[piece]
        there = place(piece)
        pltpu.make_async_remote_copy(
            src_ref=there, dst_ref=there, send_sem=send_sem.at[n], recv_sem=recv_sem.at[n],
            device_id=devices[copies[n][0]], device_id_type=MESH,
        ).wait_recv()

    def rank(k, carry):
        r = (k % 2 + x_hi) % 2 * RING + (k // 2 - z + RING) % RING
        c = (k // RING + x_lo) % 2 * RING + (k % RING - y + RING) % RING
        late = 0
        for rows, cols in turns[:-1]:
            late = late + 1 - ((rows >> r) % 2) * ((cols >> c) % 2)
        turn_ref[k] = late
        return carry

    def multiply(now):
        def step(k, carry):
            @pl.when(turn_ref[k] == now)
            def _():
                left = jnp.concatenate([rows_ref[2 * k], rows_ref[2 * k + 1]], axis=1)
                total_ref[...] += jnp.dot(left, cols_ref[k], preferred_element_type=jnp.float32)

            return carry

        lax.fori_loop(0, cols_ref.shape[0], step, 0)

    order = {piece: n for n, piece in enumerate(copy[2] for copy in copies)}
    turns, started, now = [step[1:] for step in STEPS if step[0] == "mul"], [], 0
    for step in STEPS:
        if step[0] == "mul":
            _, rows, cols = step
            ready = [p for p in order if ((rows if p[0] == "R" else cols) >> (RING * p[1] + p[2] % RING)) % 2]
            for piece in ready:
                arrive(piece)
            if now == 0:
                total_ref[...] = jnp.zeros_like(total_ref)
                lax.fori_loop(0, cols_ref.shape[0], rank, 0)
            multiply(now)
            now += 1
            continue
        n = len(started)
        flow, source, _ = copies[n]
        if flow == "sib":
            for s in range(source[-1][0], sum(source[-1])):
                arrive((*source[:-1], s))
        else:
            arrive(source)
        here = place(source)
        copy = pltpu.make_async_remote_copy(
            src_ref=here, dst_ref=here, send_sem=send_sem.at[n], recv_sem=recv_sem.at[n],
            device_id=devices[flow], device_id_type=MESH,
        )
        copy.start()
        started.append(copy)
        if n >= LAG:
            started[n - LAG].wait_send()
    out_ref[...] = total_ref[...] * cols_ref[row].astype(jnp.float32)
    for copy in started[-LAG:]:
        copy.wait_send()


def shards(edge_values, tile_pattern):
    height, breadth = edge_values.shape
    count = len(copies_of(STEPS))
    return pl.pallas_call(
        kernel,
        out_shape=jax.ShapeDtypeStruct((height, breadth), jnp.float32),
        in_specs=[pl.BlockSpec(memory_space=pl.ANY), pl.BlockSpec(memory_space=pl.ANY)],
        out_specs=pl.BlockSpec(memory_space=pltpu.VMEM),
        scratch_shapes=[
            pltpu.VMEM((height, breadth), edge_values.dtype),
            pltpu.SMEM(tile_pattern.shape[::-1], tile_pattern.dtype),
            pltpu.SMEM((16,), jnp.int32),
            pltpu.VMEM((32, height, breadth), jnp.bfloat16),
            pltpu.VMEM((16, height, breadth), jnp.bfloat16),
            pltpu.VMEM((height, breadth), jnp.float32),
            pltpu.SemaphoreType.DMA((2,)),
            pltpu.SemaphoreType.DMA((count,)),
            pltpu.SemaphoreType.DMA((count,)),
        ],
        compiler_params=pltpu.CompilerParams(
            collective_id=0, has_side_effects=True, vmem_limit_bytes=60 * 1024 * 1024
        ),
        cost_estimate=pl.CostEstimate(flops=2 * height * 8192 * breadth, bytes_accessed=1 << 20, transcendentals=0),
    )(edge_values, tile_pattern.T)


def solution(mesh):
    return jax.shard_map(
        shards,
        mesh=mesh,
        in_specs=(P("row", ("col", "layer")), P("row", ("col", "layer"))),
        out_specs=P("row", ("col", "layer")),
        check_vma=False,
    )
```

time: 57.7 us -> 55.7 us (0.965)
  Pallas kernels: 54.4 us -> 53.6 us
  local copies, waits for them, and re-layouts: 2.51 us -> 1.87 us
    pallas_call x1, Pallas kernels: 54.4 us -> 53.6 us  [shards(): pl.pallas_call(kernel, out_shape=jax.ShapeDtypeStruct((height, breadth),...]
    unnamed x4 -> x1, local copies, waits for them, and re-layouts: 2.51 us -> 1.87 us
where the time goes in v3:
time: 55.7 us; the launch traced here: 55.5 us
  Pallas kernels  53.6 us (96%)
  local copies, waits for them, and re-layouts  1.87 us (3%)
    pallas_call x1, Pallas kernels, shards(): pl.pallas_call(kernel, out_shape=jax.ShapeDtypeStruct((height, breadth),...  53.6 us
    unnamed x1, local copies, waits for them, and re-layouts  1.87 us

profile of v3, /device:TPU:1, one launch (start us, length us, event | category | flops | bytes accessed | tf_op | source)
XLA Modules:
  0.0 55.5 jit_solution(2284832283088730019)
XLA Ops:
  0.0 53.6 %shard_map.28 = f32[512,256]{1,0:T(8,128)} custom-call(bf16[512,256]{1,0:T(8,128)(2,1)} %edge_hbm.1, s32[2,4]{1,0:T(2,128)} %bitcast.1), custom_call_target="tpu_custom_call" | custom-call | flops 2147483648 | bytes 1048576 | tf_op jit(solution)/shard_map/pallas_call | solution.py:193
  53.6 1.9 %copy.4 = f32[512,256]{1,0:T(8,128)} copy(f32[512,256]{1,0:T(8,128)} %shard_map.28) | data formatting | bytes 1048576

commit v4 on v3

--- a/solution.py
+++ b/solution.py
@@ -207,10 +207,10 @@
             pltpu.SemaphoreType.DMA((count,)),
         ],
         compiler_params=pltpu.CompilerParams(
-            collective_id=0, has_side_effects=True, vmem_limit_bytes=60 * 1024 * 1024
+            collective_id=0, has_side_effects=True, vmem_limit_bytes=24 * 1024 * 1024
         ),
         cost_estimate=pl.CostEstimate(flops=2 * height * 8192 * breadth, bytes_accessed=1 << 20, transcendentals=0),
-    )(edge_values, tile_pattern.T)
+    )(*(pltpu.with_memory_space_constraint(x, pltpu.HBM) for x in (edge_values, tile_pattern.T)))
 
 
 def solution(mesh):

time: 55.7 us -> 53.8 us (0.966)
  local copies, waits for them, and re-layouts: 1.87 us -> 0.8 us
  Pallas kernels: 53.6 us -> 52.9 us
    unnamed x1, local copies, waits for them, and re-layouts: 1.87 us -> 0.8 us
    pallas_call x1, Pallas kernels: 53.6 us -> 52.9 us  [shards(): pl.pallas_call(kernel, out_shape=jax.ShapeDtypeStruct((height, breadth),...]
where the time goes in v4:
time: 53.8 us; the launch traced here: 53.7 us
  Pallas kernels  52.9 us (98%)
  local copies, waits for them, and re-layouts  0.8 us (1%)
    pallas_call x1, Pallas kernels, shards(): pl.pallas_call(kernel, out_shape=jax.ShapeDtypeStruct((height, breadth),...  52.9 us

profile of v4, /device:TPU:1, one launch (start us, length us, event | category | flops | bytes accessed | tf_op | source)
XLA Modules:
  0.0 53.7 jit_solution(3343643481113394068)
XLA Ops:
  0.0 52.9 %shard_map.28 = f32[512,256]{1,0:T(8,128)S(1)} custom-call(bf16[512,256]{1,0:T(8,128)(2,1)} %edge_hbm.1, s32[2,4]{1,0:T(2,128)} %bitcast.1), custom_call_target="tpu_custom_call" | custom-call | flops 2147483648 | bytes 1048576 | tf_op jit(solution)/shard_map/pallas_call | solution.py:193
  52.9 0.8 %copy.4 = f32[512,256]{1,0:T(8,128)} copy(f32[512,256]{1,0:T(8,128)S(1)} %shard_map.28) | data formatting | bytes 1048576

commit v5 on v4

--- a/solution.py
+++ b/solution.py
@@ -7,8 +7,9 @@
 
 MESH = pl.DeviceIdType.MESH
 RING = 8
+BLOCKS = 16
 CUTS = (0, 128, 256, 384, 512)
-LAG = 64
+LAG, LAST = 28, 8
 FLOWS = {
     "ym": ("C", 0, 1), "yp": ("C", 0, -1), "lo": ("C", 1, 0),
     "zm": ("R", 0, 1), "zp": ("R", 0, -1), "hi": ("R", 1, 0),
@@ -18,30 +19,29 @@
     ("yp", 0, 0, 1), ("zm", 0, 0, 1), ("zp", 0, 0, 1), ("lo", 0, 0, 1), ("ym", 0, 0, 2), ("yp", 0, 0, 2),
     ("zm", 0, 0, 2), ("zp", 0, 0, 2), ("lo", 0, 0, 2), ("ym", 0, 0, 3), ("yp", 0, 0, 3), ("zm", 0, 0, 3),
     ("zp", 0, 0, 3), ("lo", 0, 0, 3), ("sib", 0, 0, 0, 4), ("hi", 0, 0, 0), ("ym", 0, 1, 0), ("yp", 0, -1, 0),
-    ("zm", 0, 1, 0), ("zp", 0, -1, 0), ("ym", 1, 0, 0), ("yp", 1, 0, 0), ("hi", 0, -1, 0), ("zm", 0, 1, 1),
-    ("zp", 0, -1, 1), ("ym", 1, 0, 1), ("yp", 1, 0, 1), ("hi", 0, -1, 1), ("zm", 0, 1, 2), ("zp", 0, -1, 2),
-    ("ym", 1, 0, 2), ("yp", 1, 0, 2), ("hi", 0, -1, 2), ("sib", 0, 1, 0, 4), ("zm", 0, 1, 3), ("sib", 0, -1, 0, 4),
-    ("zp", 0, -1, 3), ("ym", 1, 0, 3), ("yp", 1, 0, 3), ("hi", 0, -1, 3), ("zm", 0, 2, 0), ("zp", 0, -2, 0),
-    ("ym", 0, 2, 0), ("yp", 0, -2, 0), ("lo", 0, -2, 0), ("zm", 1, 0, 0), ("zp", 0, -2, 1), ("ym", 0, 1, 1),
-    ("yp", 0, -1, 1), ("zm", 0, 2, 1), ("hi", 0, 2, 0), ("zp", 1, -1, 0), ("mul", 131, 387), ("ym", 0, 1, 2),
-    ("yp", 1, -1, 1), ("zm", 0, 2, 2), ("zp", 0, -2, 2), ("hi", 0, 2, 1), ("sib", 0, 2, 0, 4), ("sib", 0, -2, 0, 4),
-    ("ym", 0, 1, 3), ("yp", 1, -1, 2), ("zm", 1, -1, 1), ("zp", 1, -1, 1), ("hi", 0, 2, 2), ("sib", 0, -3, 0, 1),
-    ("ym", 1, 1, 0), ("yp", 0, -1, 2), ("zm", 1, -1, 2), ("mul", 131, 33667), ("zp", 1, -1, 2), ("hi", 0, 2, 3),
-    ("sib", 1, -1, 0, 4), ("sib", 0, -3, 1, 1), ("ym", 0, 3, 0), ("yp", 1, -1, 3), ("zm", 1, -1, 3),
-    ("zp", 1, -1, 3), ("hi", 0, -3, 0), ("ym", 0, 2, 1), ("yp", 0, -2, 1), ("zm", 0, 2, 3), ("zp", 0, -3, 0),
-    ("lo", 0, -3, 0), ("sib", 0, -3, 2, 1), ("ym", 0, 2, 2), ("mul", 32967, 33667), ("yp", 0, -1, 3),
-    ("zm", 1, 2, 0), ("zp", 0, -3, 1), ("hi", 0, -3, 1), ("ym", 0, 2, 3), ("yp", 1, -2, 1), ("zm", 1, 2, 1),
-    ("zp", 1, 2, 1), ("hi", 0, -3, 2), ("ym", 1, 1, 1), ("yp", 0, -2, 2), ("zm", 1, 2, 2), ("mul", 32967, 33671),
-    ("zp", 1, 2, 2), ("lo", 0, 2, 2), ("sib", 1, 2, 0, 4), ("sib", 1, 0, 0, 4), ("sib", 1, -2, 0, 4),
-    ("ym", 1, 1, 3), ("yp", 1, -2, 2), ("zm", 1, 2, 3), ("zp", 1, -2, 3), ("lo", 0, 4, 0), ("sib", 0, 3, 0, 4),
-    ("sib", 0, 4, 0, 1), ("ym", 0, 3, 1), ("yp", 1, -2, 3), ("zm", 1, 0, 3), ("zp", 0, -3, 2), ("hi", 0, 4, 0),
-    ("mul", 32967, 50055), ("sib", 0, 4, 1, 1), ("ym", 0, 3, 2), ("yp", 0, -2, 3), ("zm", 0, 3, 3),
-    ("zp", 0, -2, 3), ("hi", 0, 4, 1), ("ym", 0, 3, 3), ("yp", 1, -3, 1), ("lo", 0, 3, 0), ("zp", 1, -3, 2),
-    ("mul", 50639, 50127), ("ym", 1, 2, 1), ("lo", 0, 3, 2), ("yp", 1, -3, 2), ("sib", 1, 3, 0, 4),
-    ("zm", 1, 3, 3), ("sib", 1, -3, 0, 4), ("mul", 50639, 50127), ("ym", 1, 2, 3), ("yp", 1, -3, 3),
-    ("sib", 1, 1, 0, 4), ("sib", 0, 4, 2, 1), ("mul", 50639, 59343), ("sib", 1, 4, 0, 1), ("sib", 0, 4, 3, 1),
-    ("sib", 0, -3, 3, 1), ("sib", 1, 4, 1, 1), ("sib", 1, 4, 3, 1), ("sib", 1, 4, 2, 1), ("mul", 61391, 59375),
-    ("mul", 61439, 59391), ("mul", 65535, 65535),
+    ("zm", 0, 1, 0), ("zp", 0, -1, 0), ("ym", 1, 0, 0), ("yp", 1, 0, 0), ("hi", 0, 1, 0), ("zm", 0, 1, 1),
+    ("ym", 0, 1, 1), ("zp", 0, -1, 1), ("yp", 0, -1, 1), ("hi", 0, 1, 1), ("zm", 0, 1, 2), ("zp", 0, -1, 2),
+    ("ym", 1, 0, 1), ("yp", 0, -1, 2), ("lo", 0, -1, 1), ("sib", 0, 1, 0, 4), ("zm", 0, 1, 3), ("sib", 0, -1, 0, 4),
+    ("zp", 0, -1, 3), ("ym", 1, 0, 2), ("yp", 0, -1, 3), ("hi", 0, 1, 2), ("zm", 0, 2, 0), ("zp", 0, -2, 0),
+    ("ym", 1, 0, 3), ("yp", 1, 0, 2), ("hi", 0, 1, 3), ("zp", 1, 0, 0), ("zm", 0, 2, 1), ("ym", 1, 1, 0),
+    ("yp", 1, 0, 3), ("zp", 0, -2, 1), ("hi", 0, -2, 0), ("zm", 1, 1, 0), ("mul", 131, 387), ("ym", 0, 1, 2),
+    ("yp", 0, -2, 0), ("zm", 0, 2, 2), ("zp", 0, -2, 2), ("hi", 0, -2, 1), ("sib", 0, 2, 0, 4), ("ym", 1, 1, 1),
+    ("sib", 0, -2, 0, 4), ("yp", 0, -2, 1), ("zm", 0, 2, 3), ("zp", 1, 1, 1), ("hi", 0, -2, 2), ("ym", 1, 1, 2),
+    ("yp", 0, -2, 2), ("zm", 1, 1, 1), ("zp", 0, -3, 0), ("hi", 0, 3, 0), ("mul", 131, 451), ("ym", 1, 1, 3),
+    ("yp", 0, -2, 3), ("zm", 1, 1, 2), ("zp", 1, 1, 2), ("hi", 0, 3, 1), ("sib", 1, 1, 0, 4), ("ym", 0, 1, 3),
+    ("yp", 1, -1, 0), ("zm", 1, 1, 3), ("zp", 1, 1, 3), ("hi", 0, -2, 3), ("ym", 1, 2, 0), ("yp", 0, -3, 0),
+    ("zm", 0, 3, 1), ("zp", 1, -2, 0), ("hi", 0, 3, 2), ("mul", 199, 33731), ("sib", 0, 3, 0, 4),
+    ("ym", 1, 2, 1), ("yp", 0, -3, 1), ("zm", 1, -2, 1), ("zp", 1, -2, 1), ("hi", 0, 3, 3), ("ym", 1, 2, 2),
+    ("yp", 0, -3, 2), ("zm", 1, -2, 2), ("zp", 1, -2, 2), ("lo", 0, -3, 0), ("mul", 711, 33731), ("ym", 1, 2, 3),
+    ("yp", 0, -3, 3), ("zm", 0, 3, 2), ("zp", 0, -2, 3), ("lo", 0, -3, 1), ("sib", 1, 2, 0, 4), ("ym", 0, 2, 0),
+    ("sib", 1, 0, 0, 4), ("yp", 1, -1, 1), ("zm", 0, 3, 3), ("zp", 1, 0, 3), ("lo", 0, -3, 2), ("mul", 719, 34791),
+    ("sib", 1, -2, 0, 4), ("ym", 1, 3, 0), ("sib", 1, -3, 0, 1), ("yp", 1, -1, 2), ("zm", 1, 3, 0),
+    ("zp", 1, -2, 3), ("lo", 0, -3, 3), ("ym", 1, 3, 1), ("sib", 1, -3, 1, 1), ("yp", 0, 4, 1), ("zm", 1, 3, 1),
+    ("lo", 0, -2, 3), ("sib", 1, 3, 0, 4), ("mul", 18383, 34791), ("ym", 1, 3, 2), ("sib", 1, -3, 2, 1),
+    ("zp", 1, -3, 2), ("yp", 0, 4, 2), ("zm", 1, 3, 3), ("lo", 0, 4, 3), ("ym", 0, 2, 3), ("sib", 0, -3, 0, 4),
+    ("mul", 18383, 34791), ("sib", 0, 4, 0, 4), ("sib", 1, -1, 0, 4), ("mul", 20431, 36855), ("sib", 1, 4, 0, 1),
+    ("sib", 1, -3, 3, 1), ("sib", 1, 4, 1, 1), ("sib", 1, 4, 2, 1), ("mul", 20479, 45047), ("sib", 1, 4, 3, 1),
+    ("mul", 61439, 61431), ("mul", 65535, 65535),
 )
 
 
@@ -61,6 +61,19 @@
             core = (0,) if kind == "R" else ()
             copies.append((flow, (kind, side, d, *core, s), (kind, side ^ flip, wrap(d + shift), *core, s)))
     return copies
+
+
+def most_left(rows, cols):
+    counts = []
+    for n in range(4 * RING * RING):
+        x_lo, x_hi, y, z = n % 2, n // 2 % 2, n // 4 % RING, n // 4 // RING
+        left = 0
+        for k in range(BLOCKS):
+            r = (k % 2 + x_hi) % 2 * RING + (k // 2 - z) % RING
+            c = (k // RING + x_lo) % 2 * RING + (k % RING - y) % RING
+            left += 1 - ((rows >> r) % 2) * ((cols >> c) % 2)
+        counts.append(left)
+    return max(counts)
 
 
 def kernel(edge_hbm, tile_hbm, out_ref, edge_ref, tile_ref, turn_ref, rows_ref, cols_ref, total_ref, load_sem, send_sem, recv_sem):
@@ -150,20 +163,49 @@
 
             return carry
 
-        lax.fori_loop(0, cols_ref.shape[0], step, 0)
+        lax.fori_loop(0, BLOCKS, step, 0)
+
+    def picks(rows, cols):
+        packed, base = 0 * row, 0 * row + 1
+        for k in range(BLOCKS):
+            r = (k % 2 + x_hi) % 2 * RING + (k // 2 - z + RING) % RING
+            c = (k // RING + x_lo) % 2 * RING + (k % RING - y + RING) % RING
+            hit = 1 - ((rows >> r) % 2) * ((cols >> c) % 2)
+            packed = packed + hit * base * (k + 1)
+            base = base * (1 + 31 * hit)
+        return [(packed // 32**i % 32 + BLOCKS) % (BLOCKS + 1) for i in range(most_left(rows, cols))]
+
+    def finish(slots):
+        half = height // 2
+        for m in range(2):
+            span = pl.ds(m * half, half)
+            total = total_ref[span, :]
+            for slot in slots:
+                k = slot % BLOCKS
+                left = jnp.concatenate([rows_ref[2 * k, span, :], rows_ref[2 * k + 1, span, :]], axis=1)
+                total += jnp.dot(left, cols_ref[slot], preferred_element_type=jnp.float32)
+            out_ref[span, :] = total * cols_ref[row, span, :].astype(jnp.float32)
 
     order = {piece: n for n, piece in enumerate(copy[2] for copy in copies)}
     turns, started, now = [step[1:] for step in STEPS if step[0] == "mul"], [], 0
     for step in STEPS:
         if step[0] == "mul":
             _, rows, cols = step
+            if now == len(turns) - 1:
+                for copy in started[-LAG:-LAST]:
+                    copy.wait_send()
+                slots = picks(*turns[-2])
             ready = [p for p in order if ((rows if p[0] == "R" else cols) >> (RING * p[1] + p[2] % RING)) % 2]
             for piece in ready:
                 arrive(piece)
             if now == 0:
                 total_ref[...] = jnp.zeros_like(total_ref)
-                lax.fori_loop(0, cols_ref.shape[0], rank, 0)
-            multiply(now)
+                cols_ref[BLOCKS] = jnp.zeros((height, breadth), cols_ref.dtype)
+                lax.fori_loop(0, BLOCKS, rank, 0)
+            if now == len(turns) - 1:
+                finish(slots)
+            else:
+                multiply(now)
             now += 1
             continue
         n = len(started)
@@ -182,8 +224,7 @@
         started.append(copy)
         if n >= LAG:
             started[n - LAG].wait_send()
-    out_ref[...] = total_ref[...] * cols_ref[row].astype(jnp.float32)
-    for copy in started[-LAG:]:
+    for copy in started[-LAST:]:
         copy.wait_send()
 
 
@@ -198,9 +239,9 @@
         scratch_shapes=[
             pltpu.VMEM((height, breadth), edge_values.dtype),
             pltpu.SMEM(tile_pattern.shape[::-1], tile_pattern.dtype),
-            pltpu.SMEM((16,), jnp.int32),
+            pltpu.SMEM((BLOCKS,), jnp.int32),
             pltpu.VMEM((32, height, breadth), jnp.bfloat16),
-            pltpu.VMEM((16, height, breadth), jnp.bfloat16),
+            pltpu.VMEM((BLOCKS + 1, height, breadth), jnp.bfloat16),
             pltpu.VMEM((height, breadth), jnp.float32),
             pltpu.SemaphoreType.DMA((2,)),
             pltpu.SemaphoreType.DMA((count,)),

time: 53.8 us -> 53.3 us (level)
  Pallas kernels: 52.9 us -> 52.3 us
where the time goes in v5:
time: 53.3 us; the launch traced here: 53.1 us
  Pallas kernels  52.3 us (98%)
  local copies, waits for them, and re-layouts  0.8 us (2%)
    pallas_call x1, Pallas kernels, shards(): pl.pallas_call(kernel, out_shape=jax.ShapeDtypeStruct((height, breadth),...  52.3 us

profile of v5, /device:TPU:1, one launch (start us, length us, event | category | flops | bytes accessed | tf_op | source)
XLA Modules:
  0.0 53.1 jit_solution(893281126758581790)
XLA Ops:
  0.0 52.3 %shard_map.28 = f32[512,256]{1,0:T(8,128)S(1)} custom-call(bf16[512,256]{1,0:T(8,128)(2,1)} %edge_hbm.1, s32[2,4]{1,0:T(2,128)} %bitcast.1), custom_call_target="tpu_custom_call" | custom-call | flops 2147483648 | bytes 1048576 | tf_op jit(solution)/shard_map/pallas_call | solution.py:234
  52.3 0.8 %copy.4 = f32[512,256]{1,0:T(8,128)} copy(f32[512,256]{1,0:T(8,128)S(1)} %shard_map.28) | data formatting | bytes 1048576

commit v6 on v5

--- a/solution.py
+++ b/solution.py
@@ -40,7 +40,7 @@
     ("lo", 0, -2, 3), ("sib", 1, 3, 0, 4), ("mul", 18383, 34791), ("ym", 1, 3, 2), ("sib", 1, -3, 2, 1),
     ("zp", 1, -3, 2), ("yp", 0, 4, 2), ("zm", 1, 3, 3), ("lo", 0, 4, 3), ("ym", 0, 2, 3), ("sib", 0, -3, 0, 4),
     ("mul", 18383, 34791), ("sib", 0, 4, 0, 4), ("sib", 1, -1, 0, 4), ("mul", 20431, 36855), ("sib", 1, 4, 0, 1),
-    ("sib", 1, -3, 3, 1), ("sib", 1, 4, 1, 1), ("sib", 1, 4, 2, 1), ("mul", 20479, 45047), ("sib", 1, 4, 3, 1),
+    ("sib", 1, -3, 3, 1), ("sib", 1, 4, 1, 1), ("sib", 1, 4, 2, 1), ("sib", 1, 4, 3, 1), ("mul", 20479, 45047),
     ("mul", 61439, 61431), ("mul", 65535, 65535),
 )
 

time: 53.3 us -> 52.9 us (level)
  no operation moved by 1% of the time
where the time goes in v6:
time: 52.9 us; the launch traced here: 52.8 us
  Pallas kernels  52 us (98%)
  local copies, waits for them, and re-layouts  0.8 us (2%)
    pallas_call x1, Pallas kernels, shards(): pl.pallas_call(kernel, out_shape=jax.ShapeDtypeStruct((height, breadth),...  52 us

profile of v6, /device:TPU:1, one launch (start us, length us, event | category | flops | bytes accessed | tf_op | source)
XLA Modules:
  0.0 52.8 jit_solution(8912483587048855005)
XLA Ops:
  0.0 52.0 %shard_map.28 = f32[512,256]{1,0:T(8,128)S(1)} custom-call(bf16[512,256]{1,0:T(8,128)(2,1)} %edge_hbm.1, s32[2,4]{1,0:T(2,128)} %bitcast.1), custom_call_target="tpu_custom_call" | custom-call | flops 2147483648 | bytes 1048576 | tf_op jit(solution)/shard_map/pallas_call | solution.py:234
  52.0 0.8 %copy.4 = f32[512,256]{1,0:T(8,128)} copy(f32[512,256]{1,0:T(8,128)S(1)} %shard_map.28) | data formatting | bytes 1048576

commit v7 on v6

--- a/solution.py
+++ b/solution.py
@@ -39,8 +39,8 @@
     ("zp", 1, -2, 3), ("lo", 0, -3, 3), ("ym", 1, 3, 1), ("sib", 1, -3, 1, 1), ("yp", 0, 4, 1), ("zm", 1, 3, 1),
     ("lo", 0, -2, 3), ("sib", 1, 3, 0, 4), ("mul", 18383, 34791), ("ym", 1, 3, 2), ("sib", 1, -3, 2, 1),
     ("zp", 1, -3, 2), ("yp", 0, 4, 2), ("zm", 1, 3, 3), ("lo", 0, 4, 3), ("ym", 0, 2, 3), ("sib", 0, -3, 0, 4),
-    ("mul", 18383, 34791), ("sib", 0, 4, 0, 4), ("sib", 1, -1, 0, 4), ("mul", 20431, 36855), ("sib", 1, 4, 0, 1),
-    ("sib", 1, -3, 3, 1), ("sib", 1, 4, 1, 1), ("sib", 1, 4, 2, 1), ("sib", 1, 4, 3, 1), ("mul", 20479, 45047),
+    ("mul", 18383, 34791), ("sib", 0, 4, 0, 4), ("sib", 1, -1, 0, 4), ("sib", 1, 4, 0, 1), ("sib", 1, -3, 3, 1),
+    ("mul", 20431, 36855), ("sib", 1, 4, 1, 1), ("sib", 1, 4, 2, 1), ("sib", 1, 4, 3, 1), ("mul", 20479, 45047),
     ("mul", 61439, 61431), ("mul", 65535, 65535),
 )
 

time: 52.9 us -> 52.7 us (level)
  no operation moved by 1% of the time
where the time goes in v7:
time: 52.7 us; the launch traced here: 52.6 us
  Pallas kernels  51.8 us (98%)
  local copies, waits for them, and re-layouts  0.8 us (2%)
    pallas_call x1, Pallas kernels, shards(): pl.pallas_call(kernel, out_shape=jax.ShapeDtypeStruct((height, breadth),...  51.8 us

profile of v7, /device:TPU:1, one launch (start us, length us, event | category | flops | bytes accessed | tf_op | source)
XLA Modules:
  0.0 52.6 jit_solution(9389497231008267313)
XLA Ops:
  0.0 51.8 %shard_map.28 = f32[512,256]{1,0:T(8,128)S(1)} custom-call(bf16[512,256]{1,0:T(8,128)(2,1)} %edge_hbm.1, s32[2,4]{1,0:T(2,128)} %bitcast.1), custom_call_target="tpu_custom_call" | custom-call | flops 2147483648 | bytes 1048576 | tf_op jit(solution)/shard_map/pallas_call | solution.py:234
  51.8 0.8 %copy.4 = f32[512,256]{1,0:T(8,128)} copy(f32[512,256]{1,0:T(8,128)S(1)} %shard_map.28) | data formatting | bytes 1048576
